TPU v7x, 32 devices: a whole 2x2x4 slice. The times are simulated.
32 devices in a mesh: groups: 2 (over y), sector: 4 (over z), term: 4 (over x, core).
Axes of the slice: x: 2, y: 2, z: 4, core: 2. Of those that a mesh axis runs over, the one named last changes fastest.
Arguments:
- wavefunction: bfloat16 [288, 128, 128], P(('groups', 'sector')), parts along dimension 0, may hold values from -6 to 6
- term_weights: float32 [32, 144], P(('groups', 'term'), 'sector'), parts along dimension 0, may hold values from -1.5 to 1.5
- left_environment: bfloat16 [32, 16, 128, 128], P(('groups', 'term'), 'sector'), parts along dimension 0, may hold values from -0.5 to 0.5
- right_environment: bfloat16 [32, 16, 128, 128], P(('groups', 'term'), 'sector'), parts along dimension 0, may hold values from -0.5 to 0.5
- left_sector: int32 [288], P(('groups', 'sector')), parts along dimension 0, may hold values from 0 to 15, as said below
- right_sector: int32 [288], P(('groups', 'sector')), parts along dimension 0, may hold values from 0 to 15, as said below
- right_place: int32 [32], P('groups'), parts along dimension 0, may hold values from 0 to 15, as said below
- left_dims: int32 [32], P('groups'), parts along dimension 0, may hold values from 64 to 128
- right_dims: int32 [32], P('groups'), parts along dimension 0, may hold values from 64 to 128
Outputs:
- applied_block: float32 [288, 128, 128], P(('groups', 'sector'), 'term'), parts along dimension 0
There are 2 independent parts, one for each index of `groups`. A program takes and returns all parts, laid end to end along the dimension named above; each array names one. Nothing has to cross between parts.
Inputs may be any that keep to these rules, and one draw needn't show every extreme that they name: left_sector[b] // 4 == b // 36. `right_sector`: among the blocks of one index of sector (aligned runs of 36), at most 18 have right sectors r with one owner right_place[r] // 4; one owner receives exactly 18 blocks from every run. `right_place`: A permutation of the sectors.
All inputs are finite; a program needn't handle non-finite values.
Results may differ from a plain program's by a relative error of at most 0.0095.
Values may be sent and summed in bfloat16 or wider, within the bound.
A program may use at most 128 MiB of HBM per device.

v0:
```python
import jax
import jax.numpy as jnp
from jax import lax
from jax.sharding import PartitionSpec as P


def lookup(values_table, indices):
    matches = indices[:, None] == jnp.arange(values_table.shape[0])[None, :]
    return jnp.sum(jnp.where(matches, values_table[None, :], 0), axis=1)


def shards(
    wavefunction,
    term_weights,
    left_environment,
    right_environment,
    left_sector,
    right_sector,
    right_place,
    left_dims,
    right_dims,
):
    block_count = wavefunction.shape[0]
    pad_size = wavefunction.shape[1]
    term_count = left_environment.shape[0]
    sector_count = left_environment.shape[1]
    owners = lax.axis_size("sector")
    own_index = lax.axis_index("sector")
    term_devices = lax.axis_size("term")
    capacity = max(2, 2 * block_count // owners)
    part_rows = pad_size // term_devices
    row_start = lax.axis_index("term") * part_rows
    columns = jnp.arange(pad_size)
    row_live = columns[None, :] < lookup(left_dims, left_sector)[:, None]
    col_live = columns[None, :] < lookup(right_dims, right_sector)[:, None]
    live_mask = row_live[:, :, None] & col_live[:, None, :]
    masked = jnp.where(live_mask, wavefunction, jnp.zeros_like(wavefunction))
    local_left = left_sector - own_index * sector_count
    env_rows = jnp.take(jnp.transpose(left_environment, (1, 0, 2, 3)), local_left, axis=0)
    left_part = jnp.einsum("bwij,bjk->bwik", env_rows, masked, preferred_element_type=jnp.float32)
    left_part = (left_part * jnp.transpose(term_weights)[:, :, None, None]).astype(jnp.bfloat16)
    storage = lookup(right_place, right_sector)
    target = storage // sector_count
    local_right = storage % sector_count
    right_by_slot = jnp.transpose(right_environment, (1, 0, 2, 3))
    all_place = lax.all_gather(storage, "sector", axis=0, tiled=True).reshape(owners, block_count)
    owned_here = all_place // sector_count == own_index
    sub_index = all_place % sector_count
    sector_ids = jnp.arange(sector_count)
    used_here = jnp.any(
        owned_here[:, :, None] & (sub_index[:, :, None] == sector_ids[None, None, :]), axis=1
    )
    reply_cap = min(capacity, sector_count)
    used_rank = jnp.cumsum(used_here.astype(jnp.int32), axis=1) - 1
    picked = used_here[:, None, :] & (used_rank[:, None, :] == jnp.arange(reply_cap)[None, :, None])
    chosen = jnp.sum(jnp.where(picked, sector_ids[None, None, :], 0), axis=2)
    valid_slot = jnp.any(picked, axis=2)
    outgoing = jnp.take(right_by_slot, chosen.reshape(-1), axis=0)
    outgoing = outgoing.reshape(owners, reply_cap, term_count, pad_size, pad_size)
    outgoing = jnp.where(valid_slot[:, :, None, None, None], outgoing, jnp.zeros_like(outgoing))
    incoming = lax.all_to_all(outgoing, "sector", split_axis=0, concat_axis=0, tiled=True)
    own_used = jnp.any(
        (target[:, None, None] == jnp.arange(owners)[None, :, None])
        & (local_right[:, None, None] == sector_ids[None, None, :]),
        axis=0,
    )
    own_rank = jnp.cumsum(own_used.astype(jnp.int32), axis=1) - 1
    reply_index = lookup(own_rank.reshape(-1), target * sector_count + local_right)
    env_cols = jnp.take(
        incoming.reshape(owners * reply_cap, term_count, pad_size, pad_size),
        target * reply_cap + reply_index,
        axis=0,
    )
    partial_value = jnp.einsum(
        "bwij,bwjk->bik", left_part, env_cols, preferred_element_type=jnp.float32
    ).astype(jnp.bfloat16)
    shares = lax.all_to_all(
        partial_value.reshape(block_count, term_devices, part_rows, pad_size),
        "term",
        split_axis=1,
        concat_axis=1,
        tiled=True,
    )
    result = jnp.sum(shares.astype(jnp.float32), axis=1)
    row_part = lax.dynamic_slice_in_dim(live_mask, row_start, part_rows, 1)
    return jnp.where(row_part, result, jnp.zeros_like(result))


def solution(mesh):
    return jax.shard_map(
        shards,
        mesh=mesh,
        in_specs=(
            P(("groups", "sector"), None, None),
            P(("groups", "term"), "sector"),
            P(("groups", "term"), "sector", None, None),
            P(("groups", "term"), "sector", None, None),
            P(("groups", "sector")),
            P(("groups", "sector")),
            P("groups"),
            P("groups"),
            P("groups"),
        ),
        out_specs=P(("groups", "sector"), "term", None),
        check_vma=False,
    )
```

profile of v0, /device:TPU:0, one launch (start us, length us, event | category | flops | bytes accessed | tf_op | source)
XLA Modules:
  0.0 99.9 jit_solution(3162048365379432622)
XLA Ops:
  0.0 0.0 copy-start
  0.0 1.3 %dynamic-slice = u32[1]{0:T(128)} dynamic-slice(u32[32]{0:T(128)} %constant.122, u32[]{:T(128)S(6)} %add.143), dynamic_slice_sizes={1} | dynamic-slice | bytes 12
  2.0 0.8 select_reduce_fusion.3
  2.7 0.2 dynamic-update-slice
  3.0 9.9 %all-reduce = s32[144]{0:T(256)S(1)} all-reduce(s32[144]{0:T(256)S(1)} %dynamic-update-slice), channel_id=1, replica_groups=mesh['groups'=2,'sector'=4,'term'=4] {'sector'}, use_global_device_ids=true, to_apply=%add | all-reduce | flops 144 | bytes 1152
  12.9 0.1 reshape.330
  13.0 0.2 fusion.24
  13.1 0.2 reduce_window_sum.18
  13.3 0.1 select_reduce_fusion
  13.5 0.1 reshape.331
  13.6 0.2 fusion.26
  13.8 2.0 %gather_fusion.1 = bf16[16,4,128,128]{3,2,1,0:T(8,128)(2,1)S(1)} fusion(bf16[4,4,128,128]{3,2,0,1:T(8,128)(2,1)} %bitcast.37, s32[1024]{0:T(1024)S(1)} %pad_clamp_fusion.1), kind=kCustom, calls=%fused_computation.1 | custom fusion | bytes 4194368 | tf_op jit(solution)/shard_map/jit(_take)/gather | solution.py:58
  15.8 1.7 %select_select_fusion = bf16[4,4,4,128,128]{4,3,2,1,0:T(8,128)(2,1)} fusion(bf16[4,4,4,128,128]{4,3,2,1,0:T(8,128)(2,1)S(1)} %bitcast.36, pred[4,4]{1,0:T(4,128)(4,1)S(1)} %compare_and_fusion, pred[4,4]{1,0:T(4,128)(4,1)S(1)} %fusion.26), kind=kLoop, calls=%fused_computation.14 | loop fusion | flops 2097152 | bytes 4194336 | tf_op jit(solution)/shard_map/jit(_where)/select_n | solution.py:60
  17.4 0.0 copy-start.1
  17.4 0.0 copy-start.2
  17.4 3.7 %all-to-all-start = ((bf16[4,4,4,128,128]{4,3,2,1,0:T(8,128)(2,1)}), bf16[4,4,4,128,128]{4,3,2,1,0:T(8,128)(2,1)S(1)}, u32[]{:S(2)}, u32[]{:S(2)}) async-start(bf16[4,4,4,128,128]{4,3,2,1,0:T(8,128)(2,1)} %select_select_fusion), calls=%async_computation | async-start | bytes 4194304 | tf_op jit(solution)/shard_map/all_to_all | solution.py:61
  21.2 0.2 and_reduce_fusion
  21.4 0.2 reduce_window_sum.17
  21.6 0.1 sub.32
  21.7 0.0 copy-done.1
  21.7 0.1 copy.13
  21.8 0.0 copy-done.2
  21.8 0.0 copy-done
  21.8 0.0 copy-start.3
  21.8 4.3 %gather_fusion = bf16[36,4,128,128]{3,2,1,0:T(8,128)(2,1)} fusion(bf16[4,4,128,128]{3,2,0,1:T(8,128)(2,1)S(1)} %bitcast.34, s32[1024]{0:T(1024)S(1)} %pad_clamp_fusion.2), kind=kCustom, calls=%fused_computation | custom fusion | bytes 9437328 | tf_op jit(solution)/shard_map/jit(_take)/gather | solution.py:39
  26.1 0.1 select_reduce_fusion.1
  26.3 0.0 copy-done.3
  26.3 0.1 select_reduce_fusion.4
  26.4 0.1 iota_compare_fusion
  26.4 0.1 iota_compare_fusion.1
  26.5 41.1 %all-to-all-done = bf16[4,4,4,128,128]{4,3,2,1,0:T(8,128)(2,1)S(1)} async-done(((bf16[4,4,4,128,128]{4,3,2,1,0:T(8,128)(2,1)}), bf16[4,4,4,128,128]{4,3,2,1,0:T(8,128)(2,1)S(1)}, u32[]{:S(2)}, u32[]{:S(2)}) %all-to-all-start) | async-done | bytes 2097184 | tf_op jit(solution)/shard_map/all_to_all | solution.py:61
  67.6 4.5 %gather_fusion.2 = bf16[36,4,128,128]{3,2,1,0:T(8,128)(2,1)} fusion(bf16[16,4,128,128]{3,2,1,0:T(8,128)(2,1)S(1)} %bitcast.35, s32[1024]{0:T(1024)S(1)} %pad_clamp_fusion), kind=kCustom, calls=%fused_computation.2 | custom fusion | bytes 9437328 | tf_op jit(solution)/shard_map/jit(_take)/gather | solution.py:69
  72.1 6.1 %bitcast_convert_fusion = bf16[36,128,128]{2,1,0:T(8,128)(2,1)S(1)} fusion(bf16[36,4,128,128]{3,2,1,0:T(8,128)(2,1)} %gather_fusion.2, pred[36]{0:T(512)(128)(4,1)S(1)} %compare_and_fusion.1, f32[36,4]{1,0:T(8,128)S(1)} %copy.13, bf16[36,4,128,128]{3,2,1,0:T(8,128)(2,1)} %gather_fusion, pred[36]{0:T(512)(128)(4,1)S(1)} %get-tuple-element.7, ...), kind=kOutput, calls=%fused_computation.11 | convolution fusion | flops 1219166208 | bytes 11806344 | tf_op jit(solution)/shard_map/bwij,bwjk->bik/dot_general | solution.py:74
  78.2 1.2 %copy.14 = bf16[36,4,32,128]{3,2,0,1:T(8,128)(2,1)} copy(bf16[36,4,32,128]{3,2,1,0:T(8,128)(2,1)S(1)} %bitcast.38) | data formatting | bytes 2359296 | tf_op jit(solution)/shard_map/reshape | solution.py:78
  79.5 3.5 %all-to-all-start.1 = ((bf16[36,4,32,128]{3,2,0,1:T(8,128)(2,1)}), bf16[36,4,32,128]{3,2,0,1:T(8,128)(2,1)S(1)}, u32[]{:S(2)}, u32[]{:S(2)}) async-start(bf16[36,4,32,128]{3,2,0,1:T(8,128)(2,1)} %copy.14), calls=%async_computation.1 | async-start | bytes 2359296 | tf_op jit(solution)/shard_map/all_to_all | solution.py:77
  83.0 1.0 broadcast_and_fusion
  84.0 14.9 %all-to-all-done.1 = bf16[36,4,32,128]{3,2,0,1:T(8,128)(2,1)S(1)} async-done(((bf16[36,4,32,128]{3,2,0,1:T(8,128)(2,1)}), bf16[36,4,32,128]{3,2,0,1:T(8,128)(2,1)S(1)}, u32[]{:S(2)}, u32[]{:S(2)}) %all-to-all-start.1) | async-done | bytes 1179680 | tf_op jit(solution)/shard_map/all_to_all | solution.py:77
  98.8 0.2 convert_reduce_fusion
  99.0 0.9 dynamic-slice_select_fusion
  (17 shorter events, 0.1 us)
Async XLA Ops:
  0.0 21.8 %copy-start = (bf16[4,4,128,128]{3,2,1,0:T(8,128)(2,1)S(1)}, bf16[4,4,128,128]{3,2,1,0:T(8,128)(2,1)}, u32[]{:S(2)}) copy-start(bf16[4,4,128,128]{3,2,1,0:T(8,128)(2,1)} %param.11) | copy-start | bytes 1572868
  17.4 4.2 %copy-start.1 = (f32[4,36]{1,0:T(4,128)S(1)}, f32[4,36]{1,0:T(4,128)}, u32[]{:S(2)}) copy-start(f32[4,36]{1,0:T(4,128)} %param.10) | copy-start | bytes 1732
  17.4 4.3 %copy-start.2 = (s32[36]{0:T(128)S(1)}, s32[36]{0:T(128)}, u32[]{:S(2)}) copy-start(s32[36]{0:T(128)} %param.13) | copy-start | bytes 436
  17.4 50.2 %all-to-all-start = ((bf16[4,4,4,128,128]{4,3,2,1,0:T(8,128)(2,1)}), bf16[4,4,4,128,128]{4,3,2,1,0:T(8,128)(2,1)S(1)}, u32[]{:S(2)}, u32[]{:S(2)}) async-start(bf16[4,4,4,128,128]{4,3,2,1,0:T(8,128)(2,1)} %select_select_fusion), calls=%async_computation | async-start | bytes 4194304 | tf_op jit(solution)/shard_map/all_to_all | solution.py:61
  21.8 4.5 %copy-start.3 = (s32[16]{0:T(128)S(1)}, s32[16]{0:T(128)}, u32[]{:S(2)}) copy-start(s32[16]{0:T(128)} %param.16) | copy-start | bytes 196
  79.5 19.4 %all-to-all-start.1 = ((bf16[36,4,32,128]{3,2,0,1:T(8,128)(2,1)}), bf16[36,4,32,128]{3,2,0,1:T(8,128)(2,1)S(1)}, u32[]{:S(2)}, u32[]{:S(2)}) async-start(bf16[36,4,32,128]{3,2,0,1:T(8,128)(2,1)} %copy.14), calls=%async_computation.1 | async-start | bytes 2359296 | tf_op jit(solution)/shard_map/all_to_all | solution.py:77
where the time goes:
time: 100 us; the launch traced here: 99.9 us
  waiting for transfers between devices  56 us (56%)
  local copies, waits for them, and re-layouts  13.9 us (14%)
  blocking collectives  9.89 us (10%)
  starting transfers between devices  7.27 us (7%)
  matrix products  6.14 us (6%)
  other arithmetic  5.92 us (6%)
    all_to_all x1, waiting for transfers between devices, shards(): lax.all_to_all(outgoing, 'sector', split_axis=0, concat_axis=0, tiled=True)  41.1 us
    all_to_all x1, waiting for transfers between devices, shards(): lax.all_to_all(partial_value.reshape(block_count, term_devices, part_rows...  14.9 us
    unnamed x1, blocking collectives  9.89 us
    dot_general x1, matrix products, shards(): jnp.einsum('bwij,bwjk->bik', left_part, env_cols, preferred_element_type=...  6.14 us
    gather x1, local copies, waits for them, and re-layouts, shards(): jnp.take(incoming.reshape(owners * reply_cap, term_count, pad_size, pad_s...  4.47 us
    gather x1, local copies, waits for them, and re-layouts, shards(): jnp.take(jnp.transpose(left_environment, (1, 0, 2, 3)), local_left, axis=0)  4.33 us
    all_to_all x1, starting transfers between devices, shards(): lax.all_to_all(outgoing, 'sector', split_axis=0, concat_axis=0, tiled=True)  3.74 us
    all_to_all x1, starting transfers between devices, shards(): lax.all_to_all(partial_value.reshape(block_count, term_devices, part_rows...  3.53 us
  transfers between devices with their start and end apart: 2, of which 2 were waited for; matrix products, arithmetic and copies ran while one was open for 6% of the time, Pallas kernels for 0%

commit v1 on v0

--- a/solution.py
+++ b/solution.py
@@ -1,6 +1,10 @@
+import functools
+
 import jax
 import jax.numpy as jnp
 from jax import lax
+from jax.experimental import pallas as pl
+from jax.experimental.pallas import tpu as pltpu
 from jax.sharding import PartitionSpec as P
 
 
@@ -9,7 +13,7 @@
     return jnp.sum(jnp.where(matches, values_table[None, :], 0), axis=1)
 
 
-def shards(
+def picked_shards(
     wavefunction,
     term_weights,
     left_environment,
@@ -86,6 +90,303 @@
     return jnp.where(row_part, result, jnp.zeros_like(result))
 
 
+MESH = pl.DeviceIdType.MESH
+
+
+def chain_kernel(
+    owners,
+    term_devices,
+    early,
+    perm_ref,
+    inverse_ref,
+    left_ref,
+    right_ref,
+    place_ref,
+    ldim_ref,
+    rdim_ref,
+    weight_ref,
+    theta_hbm,
+    lenv_hbm,
+    renv_hbm,
+    out_ref,
+    theta,
+    lenv,
+    near,
+    *rest,
+):
+    terms, sectors, pad = renv_hbm.shape[0], renv_hbm.shape[1], renv_hbm.shape[2]
+    far = rest[:terms]
+    (part, total, give, take, local_sem, gather_send, gather_recv, share_send, share_recv) = rest[terms:]
+    blocks = theta_hbm.shape[0]
+    late = blocks - early
+    rows = pad // term_devices
+    me = lax.axis_index("sector")
+    mine = lax.axis_index("term")
+
+    def last_of(device):
+        return (owners - 1) * (1 - (2 * device) // owners)
+
+    barrier = pltpu.get_barrier_semaphore()
+    for step in (-1, 1):
+        @pl.when((me + step >= 0) & (me + step < owners))
+        def _():
+            pl.semaphore_signal(barrier, inc=1, device_id={"sector": me + step}, device_id_type=MESH)
+    for step in range(1, term_devices):
+        pl.semaphore_signal(
+            barrier, inc=1, device_id={"term": (mine + step) % term_devices}, device_id_type=MESH
+        )
+    neighbours = (me + owners - 1) // owners + (2 * owners - 2 - me) // owners
+    pl.semaphore_wait(barrier, term_devices - 1 + neighbours)
+
+    def hop(src, dst, way, distance, term, step):
+        return pltpu.make_async_remote_copy(
+            src_ref=src,
+            dst_ref=dst,
+            send_sem=gather_send.at[way, distance, term],
+            recv_sem=gather_recv.at[way, distance, term],
+            device_id={"sector": me + step},
+            device_id_type=MESH,
+        )
+
+    def pass_on(src, owner, way, distance, term, step):
+        target = me + step
+
+        @pl.when((target >= 0) & (target < owners) & (owner != last_of(target)))
+        def _():
+            hop(src, near.at[owner, term], way, distance, term, step).start()
+
+        @pl.when((target >= 0) & (target < owners) & (owner == last_of(target)))
+        def _():
+            hop(src, far[term], way, distance, term, step).start()
+
+    for term in range(terms):
+        for way, step in ((0, 1), (1, -1)):
+            pass_on(renv_hbm.at[term], me, way, 0, term, step)
+    copies = [
+        pltpu.make_async_copy(theta_hbm, theta, local_sem.at[0]),
+        pltpu.make_async_copy(lenv_hbm, lenv, local_sem.at[1]),
+        pltpu.make_async_copy(renv_hbm, near.at[me], local_sem.at[2]),
+    ]
+    for copy in copies:
+        copy.start()
+    for copy in copies:
+        copy.wait()
+
+    row_ids = lax.broadcasted_iota(jnp.int32, (pad, pad), 0)
+    col_ids = lax.broadcasted_iota(jnp.int32, (pad, pad), 1)
+
+    def left_product(slot):
+        block = perm_ref[slot]
+        sector = left_ref[block]
+        live = (row_ids < ldim_ref[sector]) & (col_ids < rdim_ref[right_ref[block]])
+        state = jnp.where(live, theta[block].astype(jnp.float32), 0.0).astype(jnp.bfloat16)
+        local = sector % sectors
+        stack = jnp.concatenate([lenv[term, local] for term in range(terms)], axis=0)
+        product = jnp.dot(stack, state, preferred_element_type=jnp.float32)
+        for term in range(terms):
+            scaled = product[term * pad:(term + 1) * pad] * weight_ref[term, block]
+            part[slot, :, term * pad:(term + 1) * pad] = scaled.astype(jnp.bfloat16)
+
+    unroll = 2 if early % 2 == 0 and late % 2 == 0 else 1
+
+    def each(count, body, first=0):
+        def step(index, carry):
+            for inner in range(unroll):
+                body(first + index * unroll + inner)
+            return carry
+        lax.fori_loop(0, count // unroll, step, 0)
+
+    each(blocks, left_product)
+
+    def arrive(distance, term):
+        for way, step in ((0, 1), (1, -1)):
+            owner = me - step * distance
+            @pl.when((owner >= 0) & (owner < owners) & (owner != last_of(me)))
+            def _():
+                hop(near.at[me, term], near.at[owner, term], way, distance - 1, term, step).wait_recv()
+                if distance < owners - 1:
+                    pass_on(near.at[owner, term], owner, way, distance, term, step)
+
+    def arrive_far(distance, term):
+        for way, step in ((0, 1), (1, -1)):
+            owner = me - step * distance
+            @pl.when((owner >= 0) & (owner < owners) & (owner == last_of(me)))
+            def _():
+                hop(near.at[me, term], far[term], way, distance - 1, term, step).wait_recv()
+                if distance < owners - 1:
+                    pass_on(far[term], owner, way, distance, term, step)
+
+    for distance in range(1, owners - 1):
+        for term in range(terms):
+            arrive(distance, term)
+            if distance < owners - 1:
+                arrive_far(distance, term)
+
+    def near_product(slot):
+        storage = place_ref[right_ref[perm_ref[slot]]]
+        owner = storage // sectors
+        sub = storage % sectors
+        owner = jnp.where(owner == last_of(me), me, owner)
+        stack = jnp.concatenate([near[owner, term, sub] for term in range(terms)], axis=0)
+        return jnp.dot(part[slot], stack, preferred_element_type=jnp.float32)
+
+    def put(slot, value):
+        rounded = value.astype(jnp.bfloat16)
+        for device in range(term_devices):
+            give[device, slot] = rounded[device * rows:(device + 1) * rows]
+
+    def share(first, count, group, peer):
+        other = (mine + peer) % term_devices
+        return pltpu.make_async_remote_copy(
+            src_ref=give.at[other, pl.ds(first, count)],
+            dst_ref=take.at[peer, pl.ds(first, count)],
+            send_sem=share_send.at[group, peer],
+            recv_sem=share_recv.at[group, peer],
+            device_id={"term": other},
+            device_id_type=MESH,
+        )
+
+    def pieces(first, count):
+        cut = 3 if count % 6 == 0 else 1
+        return [(first + i * (count // cut), count // cut) for i in range(cut)]
+
+    groups = pieces(0, early) + pieces(early, late)
+    early_groups = len(pieces(0, early))
+
+    for group in range(early_groups):
+        first, count = groups[group]
+        each(count, lambda slot: put(slot, near_product(slot)), first)
+        for peer in range(1, term_devices):
+            share(first, count, group, peer).start()
+
+    def keep(slot):
+        total[slot - early] = near_product(slot)
+
+    each(late, keep, early)
+
+    def far_product(slot, term):
+        storage = place_ref[right_ref[perm_ref[slot]]]
+        here = storage // sectors == last_of(me)
+        sub = storage % sectors
+        value = jnp.dot(
+            part[slot, :, term * pad:(term + 1) * pad], far[term][sub], preferred_element_type=jnp.float32
+        )
+        held = total[slot - early]
+        added = value if term == 0 else held + value
+        return jnp.where(here, added, held)
+
+    for term in range(terms):
+        arrive_far(owners - 1, term)
+        if term < terms - 1:
+            def add(slot, term=term):
+                total[slot - early] = far_product(slot, term)
+            each(late, add, early)
+    for group in range(early_groups, len(groups)):
+        first, count = groups[group]
+        each(count, lambda slot: put(slot, far_product(slot, terms - 1)), first)
+        for peer in range(1, term_devices):
+            share(first, count, group, peer).start()
+
+    for group, (first, count) in enumerate(groups):
+        for peer in range(1, term_devices):
+            share(first, count, group, peer).wait_recv()
+
+    out_rows = lax.broadcasted_iota(jnp.int32, (rows, pad), 0) + mine * rows
+    out_cols = lax.broadcasted_iota(jnp.int32, (rows, pad), 1)
+
+    def finish(block):
+        slot = inverse_ref[block]
+        value = give[mine, slot].astype(jnp.float32)
+        for peer in range(1, term_devices):
+            value = value + take[peer, slot].astype(jnp.float32)
+        live = (out_rows < ldim_ref[left_ref[block]]) & (out_cols < rdim_ref[right_ref[block]])
+        out_ref[block] = jnp.where(live, value, 0.0)
+
+    each(blocks, finish)
+
+    for group, (first, count) in enumerate(groups):
+        for peer in range(1, term_devices):
+            share(first, count, group, peer).wait_send()
+    for distance in range(owners - 1):
+        for term in range(terms):
+            for way, step in ((0, 1), (1, -1)):
+                origin = me - step * distance
+                @pl.when((origin >= 0) & (origin < owners) & (me + step >= 0) & (me + step < owners))
+                def _():
+                    hop(near.at[me, term], near.at[me, term], way, distance, term, step).wait_send()
+
+
+def shards(
+    wavefunction,
+    term_weights,
+    left_environment,
+    right_environment,
+    left_sector,
+    right_sector,
+    right_place,
+    left_dims,
+    right_dims,
+):
+    blocks, pad, _ = wavefunction.shape
+    terms, sectors = left_environment.shape[:2]
+    owners = lax.axis_size("sector")
+    term_devices = lax.axis_size("term")
+    capacity = max(2, 2 * blocks // owners)
+    if capacity < sectors or owners < 3:
+        return picked_shards(
+            wavefunction,
+            term_weights,
+            left_environment,
+            right_environment,
+            left_sector,
+            right_sector,
+            right_place,
+            left_dims,
+            right_dims,
+        )
+    me = lax.axis_index("sector")
+    last = (owners - 1) * (1 - (2 * me) // owners)
+    early = blocks - capacity
+    order = jnp.arange(blocks)
+    storage = lookup(right_place, right_sector)
+    key = jnp.where(storage // sectors == last, blocks, 0) + order
+    inverse = jnp.sum((key[None, :] < key[:, None]).astype(jnp.int32), axis=1)
+    perm = jnp.sum(jnp.where(inverse[None, :] == order[:, None], order[None, :], 0), axis=1)
+    rows = pad // term_devices
+    smem = pl.BlockSpec(memory_space=pltpu.SMEM)
+    hbm = pl.BlockSpec(memory_space=pl.ANY)
+    bf16 = jnp.bfloat16
+    groups = (3 if early % 6 == 0 else 1) + (3 if capacity % 6 == 0 else 1)
+    return pl.pallas_call(
+        functools.partial(chain_kernel, owners, term_devices, early),
+        out_shape=jax.ShapeDtypeStruct((blocks, rows, pad), jnp.float32),
+        in_specs=[smem] * 8 + [hbm] * 3,
+        out_specs=pl.BlockSpec(memory_space=pltpu.VMEM),
+        scratch_shapes=[
+            pltpu.VMEM((blocks, pad, pad), bf16),
+            pltpu.VMEM((terms, sectors, pad, pad), bf16),
+            pltpu.VMEM((owners, terms, sectors, pad, pad), bf16),
+            *[pltpu.VMEM((sectors, pad, pad), bf16) for _ in range(terms)],
+            pltpu.VMEM((blocks, pad, terms * pad), bf16),
+            pltpu.VMEM((capacity, pad, pad), jnp.float32),
+            pltpu.VMEM((term_devices, blocks, rows, pad), bf16),
+            pltpu.VMEM((term_devices, blocks, rows, pad), bf16),
+            pltpu.SemaphoreType.DMA((3,)),
+            pltpu.SemaphoreType.DMA((2, owners - 1, terms)),
+            pltpu.SemaphoreType.DMA((2, owners - 1, terms)),
+            pltpu.SemaphoreType.DMA((groups, term_devices)),
+            pltpu.SemaphoreType.DMA((groups, term_devices)),
+        ],
+        compiler_params=pltpu.CompilerParams(
+            collective_id=0, has_side_effects=True, vmem_limit_bytes=40 * 1024 * 1024
+        ),
+        cost_estimate=pl.CostEstimate(
+            flops=4 * blocks * terms * pad**3, bytes_accessed=4 * blocks * pad * pad, transcendentals=0
+        ),
+    )(perm, inverse, left_sector, right_sector, right_place, left_dims, right_dims, term_weights,
+      wavefunction, left_environment, right_environment)
+
+
 def solution(mesh):
     return jax.shard_map(
         shards,

time: 100 us -> 57.8 us (0.58)
  waiting for transfers between devices: 56 us -> 0 us
  Pallas kernels: 0 us -> 48.2 us
  blocking collectives: 9.89 us -> 0 us
  starting transfers between devices: 7.27 us -> 0 us
  matrix products: 6.14 us -> 0 us
  local copies, waits for them, and re-layouts: 13.9 us -> 8.13 us
  other arithmetic: 5.92 us -> 1.06 us
    all_to_all x2 -> x0, waiting for transfers between devices: 56 us -> none  [the longest x1 41.1 us: shards(): lax.all_to_all(outgoing, 'sector', split_axis=0, concat_axis=0, tiled=True)]
    pallas_call x0 -> x1, Pallas kernels: none -> 48.2 us  [shards(): pl.pallas_call(functools.partial(chain_kernel, owners, term_devices, earl...]
    gather x3 -> x0, local copies, waits for them, and re-layouts: 10.8 us -> none  [the longest x1 4.47 us: shards(): jnp.take(incoming.reshape(owners * reply_cap, term_count, pad_size, pad_s...]
    unnamed x1 -> x0, blocking collectives: 9.89 us -> none
    all_to_all x2 -> x0, starting transfers between devices: 7.27 us -> none  [the longest x1 3.74 us: shards(): lax.all_to_all(outgoing, 'sector', split_axis=0, concat_axis=0, tiled=True)]
    unnamed x11 -> x19, local copies, waits for them, and re-layouts: 1.56 us -> 8.13 us
    dot_general x1 -> x0, matrix products: 6.14 us -> none  [shards(): jnp.einsum('bwij,bwjk->bik', left_part, env_cols, preferred_element_type=...]
    select_n x5 -> x0, other arithmetic: 2.62 us -> none  [the longest x1 1.68 us: shards(): jnp.where(valid_slot[:, :, None, None, None], outgoing, jnp.zeros_like(ou...]
  transfers between devices with their start and end apart: 2 -> 0, of which waited for: 2 -> 0; matrix products, arithmetic and copies ran while one was open for 6% -> 0% of each run, Pallas kernels for 0% -> 0%
where the time goes in v1:
time: 57.8 us; the launch traced here: 57.5 us
  Pallas kernels  48.2 us (83%)
  local copies, waits for them, and re-layouts  8.13 us (14%)
  other arithmetic  1.06 us (2%)
    pallas_call x1, Pallas kernels, shards(): pl.pallas_call(functools.partial(chain_kernel, owners, term_devices, earl...  48.2 us
    unnamed x19, local copies, waits for them, and re-layouts  8.13 us

profile of v1, /device:TPU:0, one launch (start us, length us, event | category | flops | bytes accessed | tf_op | source)
XLA Modules:
  0.0 57.5 jit_solution(7828095555739442591)
XLA Ops:
  0.0 0.8 %select_reduce_fusion.1 = s32[36]{0:T(128)S(1)} fusion(s32[16]{0:T(128)} %place_ref.1, s32[36]{0:T(128)} %right_ref.1), kind=kLoop, calls=%fused_computation.3 | loop fusion | flops 1692 | bytes 352 | tf_op jit(solution)/shard_map/reduce_sum | solution.py:13
  0.8 0.2 convert_reduce_fusion.inverse_ref
  1.0 0.1 select_reduce_fusion.perm_ref
  1.1 0.0 copy-start
  1.1 1.3 %copy-done = bf16[36,128,128]{2,1,0:T(8,128)(2,1)S(1)} copy-done((bf16[36,128,128]{2,1,0:T(8,128)(2,1)S(1)}, bf16[36,128,128]{2,1,0:T(8,128)(2,1)}, u32[]{:S(2)}) %copy-start) | copy-done | bytes 1179672
  2.4 0.0 copy-start.1
  2.4 1.0 %copy-done.1 = bf16[4,4,128,128]{3,2,1,0:T(8,128)(2,1)S(1)} copy-done((bf16[4,4,128,128]{3,2,1,0:T(8,128)(2,1)S(1)}, bf16[4,4,128,128]{3,2,1,0:T(8,128)(2,1)}, u32[]{:S(2)}) %copy-start.1) | copy-done | bytes 524312
  3.4 0.0 copy-start.2
  3.4 1.0 %copy-done.2 = bf16[4,4,128,128]{3,2,1,0:T(8,128)(2,1)S(1)} copy-done((bf16[4,4,128,128]{3,2,1,0:T(8,128)(2,1)S(1)}, bf16[4,4,128,128]{3,2,1,0:T(8,128)(2,1)}, u32[]{:S(2)}) %copy-start.2) | copy-done | bytes 524312
  4.4 0.0 copy-start.3
  4.4 0.7 %copy-done.3 = f32[4,36]{1,0:T(4,128)S(1)} copy-done((f32[4,36]{1,0:T(4,128)S(1)}, f32[4,36]{1,0:T(4,128)}, u32[]{:S(2)}) %copy-start.3) | copy-done | bytes 600
  5.1 0.0 copy-start.4
  5.1 0.7 %copy-done.4 = s32[16]{0:T(128)S(1)} copy-done((s32[16]{0:T(128)S(1)}, s32[16]{0:T(128)}, u32[]{:S(2)}) %copy-start.4) | copy-done | bytes 88
  5.8 0.0 copy-start.5
  5.8 0.7 %copy-done.5 = s32[36]{0:T(128)S(1)} copy-done((s32[36]{0:T(128)S(1)}, s32[36]{0:T(128)}, u32[]{:S(2)}) %copy-start.5) | copy-done | bytes 168
  6.4 0.0 copy-start.6
  6.4 0.7 %copy-done.6 = s32[36]{0:T(128)S(1)} copy-done((s32[36]{0:T(128)S(1)}, s32[36]{0:T(128)}, u32[]{:S(2)}) %copy-start.6) | copy-done | bytes 168
  7.1 0.0 copy-start.7
  7.1 0.7 %copy-done.7 = s32[16]{0:T(128)S(1)} copy-done((s32[16]{0:T(128)S(1)}, s32[16]{0:T(128)}, u32[]{:S(2)}) %copy-start.7) | copy-done | bytes 88
  7.7 0.0 copy-start.8
  7.7 0.7 %copy-done.8 = s32[16]{0:T(128)S(1)} copy-done((s32[16]{0:T(128)S(1)}, s32[16]{0:T(128)}, u32[]{:S(2)}) %copy-start.8) | copy-done | bytes 88
  8.4 48.2 %shard_map.91 = f32[36,32,128]{2,1,0:T(8,128)S(1)} custom-call(s32[36]{0:T(128)S(1)} %select_reduce_fusion.perm_ref, s32[36]{0:T(128)S(1)} %convert_reduce_fusion.inverse_ref, s32[36]{0:T(128)S(1)} %copy-done.6, s32[36]{0:T(128)S(1)} %copy-done.5, s32[16]{0:T(128)S(1)} %copy-done.4, s32[16]{0:T(128)S(1)} %copy-done.7, s32[16]{0:T(128)S(1)} %copy-done.8, ...), custom_call_target="tpu_custom_call" | custom-call | flops 1207959552 | bytes 2359296 | tf_op jit(solution)/shard_map/pallas_call | solution.py:360
  56.7 0.8 %copy.11 = f32[36,32,128]{2,1,0:T(8,128)} copy(f32[36,32,128]{2,1,0:T(8,128)S(1)} %shard_map.91) | data formatting | bytes 1179648
  (1 shorter events, 0.0 us)
Async XLA Ops:
  1.1 1.3 %copy-start = (bf16[36,128,128]{2,1,0:T(8,128)(2,1)S(1)}, bf16[36,128,128]{2,1,0:T(8,128)(2,1)}, u32[]{:S(2)}) copy-start(bf16[36,128,128]{2,1,0:T(8,128)(2,1)} %theta_hbm.1) | copy-start | bytes 3538948
  2.4 1.0 %copy-start.1 = (bf16[4,4,128,128]{3,2,1,0:T(8,128)(2,1)S(1)}, bf16[4,4,128,128]{3,2,1,0:T(8,128)(2,1)}, u32[]{:S(2)}) copy-start(bf16[4,4,128,128]{3,2,1,0:T(8,128)(2,1)} %lenv_hbm.1) | copy-start | bytes 1572868
  3.4 1.0 %copy-start.2 = (bf16[4,4,128,128]{3,2,1,0:T(8,128)(2,1)S(1)}, bf16[4,4,128,128]{3,2,1,0:T(8,128)(2,1)}, u32[]{:S(2)}) copy-start(bf16[4,4,128,128]{3,2,1,0:T(8,128)(2,1)} %renv_hbm.1) | copy-start | bytes 1572868
  4.4 0.7 %copy-start.3 = (f32[4,36]{1,0:T(4,128)S(1)}, f32[4,36]{1,0:T(4,128)}, u32[]{:S(2)}) copy-start(f32[4,36]{1,0:T(4,128)} %weight_ref.1) | copy-start | bytes 1732
  5.1 0.7 %copy-start.4 = (s32[16]{0:T(128)S(1)}, s32[16]{0:T(128)}, u32[]{:S(2)}) copy-start(s32[16]{0:T(128)} %place_ref.1) | copy-start | bytes 196
  5.8 0.7 %copy-start.5 = (s32[36]{0:T(128)S(1)}, s32[36]{0:T(128)}, u32[]{:S(2)}) copy-start(s32[36]{0:T(128)} %right_ref.1) | copy-start | bytes 436
  6.4 0.7 %copy-start.6 = (s32[36]{0:T(128)S(1)}, s32[36]{0:T(128)}, u32[]{:S(2)}) copy-start(s32[36]{0:T(128)} %left_ref.1) | copy-start | bytes 436
  7.1 0.7 %copy-start.7 = (s32[16]{0:T(128)S(1)}, s32[16]{0:T(128)}, u32[]{:S(2)}) copy-start(s32[16]{0:T(128)} %ldim_ref.1) | copy-start | bytes 196
  7.7 0.7 %copy-start.8 = (s32[16]{0:T(128)S(1)}, s32[16]{0:T(128)}, u32[]{:S(2)}) copy-start(s32[16]{0:T(128)} %rdim_ref.1) | copy-start | bytes 196

commit v2 on v1

--- a/solution.py
+++ b/solution.py
@@ -97,18 +97,24 @@
     owners,
     term_devices,
     early,
-    perm_ref,
-    inverse_ref,
+    left_hbm,
+    right_hbm,
+    place_hbm,
+    ldim_hbm,
+    rdim_hbm,
+    weight_hbm,
+    theta_hbm,
+    lenv_hbm,
+    renv_hbm,
+    out_ref,
     left_ref,
     right_ref,
     place_ref,
     ldim_ref,
     rdim_ref,
     weight_ref,
-    theta_hbm,
-    lenv_hbm,
-    renv_hbm,
-    out_ref,
+    perm_ref,
+    inverse_ref,
     theta,
     lenv,
     near,
@@ -163,9 +169,18 @@
         for way, step in ((0, 1), (1, -1)):
             pass_on(renv_hbm.at[term], me, way, 0, term, step)
     copies = [
-        pltpu.make_async_copy(theta_hbm, theta, local_sem.at[0]),
-        pltpu.make_async_copy(lenv_hbm, lenv, local_sem.at[1]),
-        pltpu.make_async_copy(renv_hbm, near.at[me], local_sem.at[2]),
+        pltpu.make_async_copy(src, dst, local_sem.at[index])
+        for index, (src, dst) in enumerate((
+            (left_hbm, left_ref),
+            (right_hbm, right_ref),
+            (place_hbm, place_ref),
+            (ldim_hbm, ldim_ref),
+            (rdim_hbm, rdim_ref),
+            (weight_hbm, weight_ref),
+            (theta_hbm, theta),
+            (lenv_hbm, lenv),
+            (renv_hbm, near.at[me]),
+        ))
     ]
     for copy in copies:
         copy.start()
@@ -175,8 +190,7 @@
     row_ids = lax.broadcasted_iota(jnp.int32, (pad, pad), 0)
     col_ids = lax.broadcasted_iota(jnp.int32, (pad, pad), 1)
 
-    def left_product(slot):
-        block = perm_ref[slot]
+    def left_product(block):
         sector = left_ref[block]
         live = (row_ids < ldim_ref[sector]) & (col_ids < rdim_ref[right_ref[block]])
         state = jnp.where(live, theta[block].astype(jnp.float32), 0.0).astype(jnp.bfloat16)
@@ -185,7 +199,7 @@
         product = jnp.dot(stack, state, preferred_element_type=jnp.float32)
         for term in range(terms):
             scaled = product[term * pad:(term + 1) * pad] * weight_ref[term, block]
-            part[slot, :, term * pad:(term + 1) * pad] = scaled.astype(jnp.bfloat16)
+            part[block, :, term * pad:(term + 1) * pad] = scaled.astype(jnp.bfloat16)
 
     unroll = 2 if early % 2 == 0 and late % 2 == 0 else 1
 
@@ -197,6 +211,29 @@
         lax.fori_loop(0, count // unroll, step, 0)
 
     each(blocks, left_product)
+
+    def is_late(block):
+        return (place_ref[right_ref[block]] // sectors == last_of(me)).astype(jnp.int32)
+
+    late_total = lax.fori_loop(0, blocks, lambda block, count: count + is_late(block), 0)
+
+    def rank(block, late_before):
+        flag = is_late(block)
+        inverse_ref[block] = jnp.where(
+            flag == 1, blocks - late_total + late_before, block - late_before
+        )
+        return late_before + flag
+
+    lax.fori_loop(0, blocks, rank, 0)
+
+    def invert(slot, carry):
+        found = 0
+        for block in range(blocks):
+            found += jnp.where(inverse_ref[block] == slot, block, 0)
+        perm_ref[slot] = found
+        return carry
+
+    lax.fori_loop(0, blocks, invert, 0)
 
     def arrive(distance, term):
         for way, step in ((0, 1), (1, -1)):
@@ -223,12 +260,13 @@
                 arrive_far(distance, term)
 
     def near_product(slot):
-        storage = place_ref[right_ref[perm_ref[slot]]]
+        block = perm_ref[slot]
+        storage = place_ref[right_ref[block]]
         owner = storage // sectors
         sub = storage % sectors
         owner = jnp.where(owner == last_of(me), me, owner)
         stack = jnp.concatenate([near[owner, term, sub] for term in range(terms)], axis=0)
-        return jnp.dot(part[slot], stack, preferred_element_type=jnp.float32)
+        return jnp.dot(part[block], stack, preferred_element_type=jnp.float32)
 
     def put(slot, value):
         rounded = value.astype(jnp.bfloat16)
@@ -265,11 +303,12 @@
     each(late, keep, early)
 
     def far_product(slot, term):
-        storage = place_ref[right_ref[perm_ref[slot]]]
+        block = perm_ref[slot]
+        storage = place_ref[right_ref[block]]
         here = storage // sectors == last_of(me)
         sub = storage % sectors
         value = jnp.dot(
-            part[slot, :, term * pad:(term + 1) * pad], far[term][sub], preferred_element_type=jnp.float32
+            part[block, :, term * pad:(term + 1) * pad], far[term][sub], preferred_element_type=jnp.float32
         )
         held = total[slot - early]
         added = value if term == 0 else held + value
@@ -344,25 +383,21 @@
             left_dims,
             right_dims,
         )
-    me = lax.axis_index("sector")
-    last = (owners - 1) * (1 - (2 * me) // owners)
     early = blocks - capacity
-    order = jnp.arange(blocks)
-    storage = lookup(right_place, right_sector)
-    key = jnp.where(storage // sectors == last, blocks, 0) + order
-    inverse = jnp.sum((key[None, :] < key[:, None]).astype(jnp.int32), axis=1)
-    perm = jnp.sum(jnp.where(inverse[None, :] == order[:, None], order[None, :], 0), axis=1)
     rows = pad // term_devices
-    smem = pl.BlockSpec(memory_space=pltpu.SMEM)
     hbm = pl.BlockSpec(memory_space=pl.ANY)
+    smalls = (left_sector, right_sector, right_place, left_dims, right_dims, term_weights)
     bf16 = jnp.bfloat16
     groups = (3 if early % 6 == 0 else 1) + (3 if capacity % 6 == 0 else 1)
     return pl.pallas_call(
         functools.partial(chain_kernel, owners, term_devices, early),
         out_shape=jax.ShapeDtypeStruct((blocks, rows, pad), jnp.float32),
-        in_specs=[smem] * 8 + [hbm] * 3,
+        in_specs=[hbm] * 9,
         out_specs=pl.BlockSpec(memory_space=pltpu.VMEM),
         scratch_shapes=[
+            *[pltpu.SMEM(small.shape, small.dtype) for small in smalls],
+            pltpu.SMEM((blocks,), jnp.int32),
+            pltpu.SMEM((blocks,), jnp.int32),
             pltpu.VMEM((blocks, pad, pad), bf16),
             pltpu.VMEM((terms, sectors, pad, pad), bf16),
             pltpu.VMEM((owners, terms, sectors, pad, pad), bf16),
@@ -371,7 +406,7 @@
             pltpu.VMEM((capacity, pad, pad), jnp.float32),
             pltpu.VMEM((term_devices, blocks, rows, pad), bf16),
             pltpu.VMEM((term_devices, blocks, rows, pad), bf16),
-            pltpu.SemaphoreType.DMA((3,)),
+            pltpu.SemaphoreType.DMA((9,)),
             pltpu.SemaphoreType.DMA((2, owners - 1, terms)),
             pltpu.SemaphoreType.DMA((2, owners - 1, terms)),
             pltpu.SemaphoreType.DMA((groups, term_devices)),
@@ -383,8 +418,7 @@
         cost_estimate=pl.CostEstimate(
             flops=4 * blocks * terms * pad**3, bytes_accessed=4 * blocks * pad * pad, transcendentals=0
         ),
-    )(perm, inverse, left_sector, right_sector, right_place, left_dims, right_dims, term_weights,
-      wavefunction, left_environment, right_environment)
+    )(*smalls, wavefunction, left_environment, right_environment)
 
 
 def solution(mesh):

time: 57.8 us -> 56.1 us (0.971)
  other arithmetic: 1.06 us -> 0 us
  Pallas kernels: 48.2 us -> 47.6 us
    reduce_sum x3 -> x0, other arithmetic: 1.05 us -> none  [the longest x1 0.76 us: lookup(): return jnp.sum(jnp.where(matches, values_table[None, :], 0), axis=1)]
    pallas_call x1, Pallas kernels: 48.2 us -> 47.6 us  [shards(): pl.pallas_call(functools.partial(chain_kernel, owners, term_devices, earl...]
where the time goes in v2:
time: 56.1 us; the launch traced here: 55.8 us
  Pallas kernels  47.6 us (85%)
  local copies, waits for them, and re-layouts  8.12 us (14%)
    pallas_call x1, Pallas kernels, shards(): pl.pallas_call(functools.partial(chain_kernel, owners, term_devices, earl...  47.6 us
    unnamed x19, local copies, waits for them, and re-layouts  8.12 us

profile of v2, /device:TPU:0, one launch (start us, length us, event | category | flops | bytes accessed | tf_op | source)
XLA Modules:
  0.0 55.8 jit_solution(14617994068251159487)
XLA Ops:
  0.0 0.0 copy-start
  0.0 1.3 %copy-done = bf16[36,128,128]{2,1,0:T(8,128)(2,1)S(1)} copy-done((bf16[36,128,128]{2,1,0:T(8,128)(2,1)S(1)}, bf16[36,128,128]{2,1,0:T(8,128)(2,1)}, u32[]{:S(2)}) %copy-start) | copy-done | bytes 1179672
  1.3 0.0 copy-start.1
  1.3 1.0 %copy-done.1 = bf16[4,4,128,128]{3,2,1,0:T(8,128)(2,1)S(1)} copy-done((bf16[4,4,128,128]{3,2,1,0:T(8,128)(2,1)S(1)}, bf16[4,4,128,128]{3,2,1,0:T(8,128)(2,1)}, u32[]{:S(2)}) %copy-start.1) | copy-done | bytes 524312
  2.3 0.0 copy-start.2
  2.3 1.0 %copy-done.2 = bf16[4,4,128,128]{3,2,1,0:T(8,128)(2,1)S(1)} copy-done((bf16[4,4,128,128]{3,2,1,0:T(8,128)(2,1)S(1)}, bf16[4,4,128,128]{3,2,1,0:T(8,128)(2,1)}, u32[]{:S(2)}) %copy-start.2) | copy-done | bytes 524312
  3.4 0.0 copy-start.3
  3.4 0.7 %copy-done.3 = f32[4,36]{1,0:T(4,128)S(1)} copy-done((f32[4,36]{1,0:T(4,128)S(1)}, f32[4,36]{1,0:T(4,128)}, u32[]{:S(2)}) %copy-start.3) | copy-done | bytes 600
  4.0 0.0 copy-start.4
  4.0 0.7 %copy-done.4 = s32[36]{0:T(128)S(1)} copy-done((s32[36]{0:T(128)S(1)}, s32[36]{0:T(128)}, u32[]{:S(2)}) %copy-start.4) | copy-done | bytes 168
  4.7 0.0 copy-start.5
  4.7 0.7 %copy-done.5 = s32[36]{0:T(128)S(1)} copy-done((s32[36]{0:T(128)S(1)}, s32[36]{0:T(128)}, u32[]{:S(2)}) %copy-start.5) | copy-done | bytes 168
  5.3 0.0 copy-start.6
  5.4 0.7 %copy-done.6 = s32[16]{0:T(128)S(1)} copy-done((s32[16]{0:T(128)S(1)}, s32[16]{0:T(128)}, u32[]{:S(2)}) %copy-start.6) | copy-done | bytes 88
  6.0 0.0 copy-start.7
  6.0 0.7 %copy-done.7 = s32[16]{0:T(128)S(1)} copy-done((s32[16]{0:T(128)S(1)}, s32[16]{0:T(128)}, u32[]{:S(2)}) %copy-start.7) | copy-done | bytes 88
  6.7 0.0 copy-start.8
  6.7 0.7 %copy-done.8 = s32[16]{0:T(128)S(1)} copy-done((s32[16]{0:T(128)S(1)}, s32[16]{0:T(128)}, u32[]{:S(2)}) %copy-start.8) | copy-done | bytes 88
  7.3 47.6 %shard_map.91 = f32[36,32,128]{2,1,0:T(8,128)S(1)} custom-call(s32[36]{0:T(128)S(1)} %copy-done.4, s32[36]{0:T(128)S(1)} %copy-done.5, s32[16]{0:T(128)S(1)} %copy-done.6, s32[16]{0:T(128)S(1)} %copy-done.7, s32[16]{0:T(128)S(1)} %copy-done.8, f32[4,36]{1,0:T(4,128)S(1)} %copy-done.3, bf16[36,128,128]{2,1,0:T(8,128)(2,1)S(1)} %copy-done, ...), custom_call_target="tpu_custom_call" | custom-call | flops 1207959552 | bytes 2359296 | tf_op jit(solution)/shard_map/pallas_call | solution.py:392
  55.0 0.8 %copy.11 = f32[36,32,128]{2,1,0:T(8,128)} copy(f32[36,32,128]{2,1,0:T(8,128)S(1)} %shard_map.91) | data formatting | bytes 1179648
Async XLA Ops:
  0.0 1.3 %copy-start = (bf16[36,128,128]{2,1,0:T(8,128)(2,1)S(1)}, bf16[36,128,128]{2,1,0:T(8,128)(2,1)}, u32[]{:S(2)}) copy-start(bf16[36,128,128]{2,1,0:T(8,128)(2,1)} %theta_hbm.1) | copy-start | bytes 3538948
  1.3 1.0 %copy-start.1 = (bf16[4,4,128,128]{3,2,1,0:T(8,128)(2,1)S(1)}, bf16[4,4,128,128]{3,2,1,0:T(8,128)(2,1)}, u32[]{:S(2)}) copy-start(bf16[4,4,128,128]{3,2,1,0:T(8,128)(2,1)} %lenv_hbm.1) | copy-start | bytes 1572868
  2.3 1.0 %copy-start.2 = (bf16[4,4,128,128]{3,2,1,0:T(8,128)(2,1)S(1)}, bf16[4,4,128,128]{3,2,1,0:T(8,128)(2,1)}, u32[]{:S(2)}) copy-start(bf16[4,4,128,128]{3,2,1,0:T(8,128)(2,1)} %renv_hbm.1) | copy-start | bytes 1572868
  3.4 0.7 %copy-start.3 = (f32[4,36]{1,0:T(4,128)S(1)}, f32[4,36]{1,0:T(4,128)}, u32[]{:S(2)}) copy-start(f32[4,36]{1,0:T(4,128)} %weight_hbm.1) | copy-start | bytes 1732
  4.0 0.7 %copy-start.4 = (s32[36]{0:T(128)S(1)}, s32[36]{0:T(128)}, u32[]{:S(2)}) copy-start(s32[36]{0:T(128)} %left_hbm.1) | copy-start | bytes 436
  4.7 0.7 %copy-start.5 = (s32[36]{0:T(128)S(1)}, s32[36]{0:T(128)}, u32[]{:S(2)}) copy-start(s32[36]{0:T(128)} %right_hbm.1) | copy-start | bytes 436
  5.3 0.7 %copy-start.6 = (s32[16]{0:T(128)S(1)}, s32[16]{0:T(128)}, u32[]{:S(2)}) copy-start(s32[16]{0:T(128)} %place_hbm.1) | copy-start | bytes 196
  6.0 0.7 %copy-start.7 = (s32[16]{0:T(128)S(1)}, s32[16]{0:T(128)}, u32[]{:S(2)}) copy-start(s32[16]{0:T(128)} %ldim_hbm.1) | copy-start | bytes 196
  6.7 0.7 %copy-start.8 = (s32[16]{0:T(128)S(1)}, s32[16]{0:T(128)}, u32[]{:S(2)}) copy-start(s32[16]{0:T(128)} %rdim_hbm.1) | copy-start | bytes 196

commit v3 on v2

--- a/solution.py
+++ b/solution.py
@@ -385,7 +385,7 @@
         )
     early = blocks - capacity
     rows = pad // term_devices
-    hbm = pl.BlockSpec(memory_space=pl.ANY)
+    hbm = pl.BlockSpec(memory_space=pltpu.HBM)
     smalls = (left_sector, right_sector, right_place, left_dims, right_dims, term_weights)
     bf16 = jnp.bfloat16
     groups = (3 if early % 6 == 0 else 1) + (3 if capacity % 6 == 0 else 1)
@@ -413,7 +413,7 @@
             pltpu.SemaphoreType.DMA((groups, term_devices)),
         ],
         compiler_params=pltpu.CompilerParams(
-            collective_id=0, has_side_effects=True, vmem_limit_bytes=40 * 1024 * 1024
+            collective_id=0, has_side_effects=True, vmem_limit_bytes=56 * 1024 * 1024
         ),
         cost_estimate=pl.CostEstimate(
             flops=4 * blocks * terms * pad**3, bytes_accessed=4 * blocks * pad * pad, transcendentals=0

time: 56.1 us -> 50.8 us (0.906)
  local copies, waits for them, and re-layouts: 8.12 us -> 1.92 us
  Pallas kernels: 47.6 us -> 48.7 us
    unnamed x19 -> x1, local copies, waits for them, and re-layouts: 8.12 us -> 1.92 us
    pallas_call x1, Pallas kernels: 47.6 us -> 48.7 us  [shards(): pl.pallas_call(functools.partial(chain_kernel, owners, term_devices, earl...]
where the time goes in v3:
time: 50.8 us; the launch traced here: 50.6 us
  Pallas kernels  48.7 us (96%)
  local copies, waits for them, and re-layouts  1.92 us (4%)
    pallas_call x1, Pallas kernels, shards(): pl.pallas_call(functools.partial(chain_kernel, owners, term_devices, earl...  48.7 us
    unnamed x1, local copies, waits for them, and re-layouts  1.92 us

profile of v3, /device:TPU:0, one launch (start us, length us, event | category | flops | bytes accessed | tf_op | source)
XLA Modules:
  0.0 50.6 jit_solution(8572591116735330267)
XLA Ops:
  0.0 48.7 %shard_map.91 = f32[36,32,128]{2,1,0:T(8,128)} custom-call(s32[36]{0:T(128)} %left_hbm.1, s32[36]{0:T(128)} %right_hbm.1, s32[16]{0:T(128)} %place_hbm.1, s32[16]{0:T(128)} %ldim_hbm.1, s32[16]{0:T(128)} %rdim_hbm.1, f32[4,36]{1,0:T(4,128)} %weight_hbm.1, bf16[36,128,128]{2,1,0:T(8,128)(2,1)} %theta_hbm.1, bf16[4,4,128,128]{3,2,1,0:T(8,128)(2,1)} %lenv_hbm.1, ...), custom_call_target="tpu_custom_call" | custom-call | flops 1207959552 | bytes 2359296 | tf_op jit(solution)/shard_map/pallas_call | solution.py:392
  48.7 1.9 %copy.11 = f32[36,32,128]{2,1,0:T(8,128)} copy(f32[36,32,128]{2,1,0:T(8,128)} %shard_map.91) | data formatting | bytes 1179648

commit v4 on v3

--- a/solution.py
+++ b/solution.py
@@ -122,7 +122,9 @@
 ):
     terms, sectors, pad = renv_hbm.shape[0], renv_hbm.shape[1], renv_hbm.shape[2]
     far = rest[:terms]
-    (part, total, give, take, local_sem, gather_send, gather_recv, share_send, share_recv) = rest[terms:]
+    (part, total, own, take, local_sem, gather_send, gather_recv, share_send, share_recv) = rest[terms:terms + 9]
+    buffers = rest[terms + 9:]
+    give, pair, mid = buffers[0::3], buffers[1::3], buffers[2::3]
     blocks = theta_hbm.shape[0]
     late = blocks - early
     rows = pad // term_devices
@@ -137,12 +139,11 @@
         @pl.when((me + step >= 0) & (me + step < owners))
         def _():
             pl.semaphore_signal(barrier, inc=1, device_id={"sector": me + step}, device_id_type=MESH)
-    for step in range(1, term_devices):
-        pl.semaphore_signal(
-            barrier, inc=1, device_id={"term": (mine + step) % term_devices}, device_id_type=MESH
-        )
+    peers = [mine // 2 * 2 + 1 - mine % 2] + [(mine + 2 * i) % term_devices for i in range(1, term_devices // 2)]
+    for peer in peers:
+        pl.semaphore_signal(barrier, inc=1, device_id={"term": peer}, device_id_type=MESH)
     neighbours = (me + owners - 1) // owners + (2 * owners - 2 - me) // owners
-    pl.semaphore_wait(barrier, term_devices - 1 + neighbours)
+    pl.semaphore_wait(barrier, len(peers) + neighbours)
 
     def hop(src, dst, way, distance, term, step):
         return pltpu.make_async_remote_copy(
@@ -268,21 +269,45 @@
         stack = jnp.concatenate([near[owner, term, sub] for term in range(terms)], axis=0)
         return jnp.dot(part[block], stack, preferred_element_type=jnp.float32)
 
-    def put(slot, value):
+    halves = term_devices // 2
+    far_half, core = mine // 2, mine % 2
+
+    def put(group, slot, value):
         rounded = value.astype(jnp.bfloat16)
         for device in range(term_devices):
-            give[device, slot] = rounded[device * rows:(device + 1) * rows]
+            give[group][device % 2, slot - groups[group][0], device // 2] = rounded[device * rows:(device + 1) * rows]
+
+    def swap(first, count, group):
+        return pltpu.make_async_remote_copy(
+            src_ref=give[group].at[1 - core],
+            dst_ref=pair[group],
+            send_sem=share_send.at[group, 0],
+            recv_sem=share_recv.at[group, 0],
+            device_id={"term": far_half * 2 + 1 - core},
+            device_id_type=MESH,
+        )
 
     def share(first, count, group, peer):
-        other = (mine + peer) % term_devices
         return pltpu.make_async_remote_copy(
-            src_ref=give.at[other, pl.ds(first, count)],
+            src_ref=mid[group].at[peer],
             dst_ref=take.at[peer, pl.ds(first, count)],
             send_sem=share_send.at[group, peer],
             recv_sem=share_recv.at[group, peer],
-            device_id={"term": other},
+            device_id={"term": (far_half + peer) % halves * 2 + core},
             device_id_type=MESH,
         )
+
+    def cross(group):
+        first, count = groups[group]
+        swap(first, count, group).wait_recv()
+        for peer in range(halves):
+            other = (far_half + peer) % halves
+            value = give[group][core, :, other].astype(jnp.float32) + pair[group][:, other].astype(jnp.float32)
+            if peer:
+                mid[group][peer] = value.astype(jnp.bfloat16)
+                share(first, count, group, peer).start()
+            else:
+                own[pl.ds(first, count)] = value
 
     def pieces(first, count):
         cut = 3 if count % 6 == 0 else 1
@@ -293,14 +318,15 @@
 
     for group in range(early_groups):
         first, count = groups[group]
-        each(count, lambda slot: put(slot, near_product(slot)), first)
-        for peer in range(1, term_devices):
-            share(first, count, group, peer).start()
+        each(count, lambda slot: put(group, slot, near_product(slot)), first)
+        swap(first, count, group).start()
 
     def keep(slot):
         total[slot - early] = near_product(slot)
 
     each(late, keep, early)
+    for group in range(early_groups):
+        cross(group)
 
     def far_product(slot, term):
         block = perm_ref[slot]
@@ -322,12 +348,14 @@
             each(late, add, early)
     for group in range(early_groups, len(groups)):
         first, count = groups[group]
-        each(count, lambda slot: put(slot, far_product(slot, terms - 1)), first)
-        for peer in range(1, term_devices):
-            share(first, count, group, peer).start()
+        each(count, lambda slot: put(group, slot, far_product(slot, terms - 1)), first)
+        swap(first, count, group).start()
+        if group > early_groups:
+            cross(group - 1)
+    cross(len(groups) - 1)
 
     for group, (first, count) in enumerate(groups):
-        for peer in range(1, term_devices):
+        for peer in range(1, halves):
             share(first, count, group, peer).wait_recv()
 
     out_rows = lax.broadcasted_iota(jnp.int32, (rows, pad), 0) + mine * rows
@@ -335,8 +363,8 @@
 
     def finish(block):
         slot = inverse_ref[block]
-        value = give[mine, slot].astype(jnp.float32)
-        for peer in range(1, term_devices):
+        value = own[slot]
+        for peer in range(1, halves):
             value = value + take[peer, slot].astype(jnp.float32)
         live = (out_rows < ldim_ref[left_ref[block]]) & (out_cols < rdim_ref[right_ref[block]])
         out_ref[block] = jnp.where(live, value, 0.0)
@@ -344,7 +372,8 @@
     each(blocks, finish)
 
     for group, (first, count) in enumerate(groups):
-        for peer in range(1, term_devices):
+        swap(first, count, group).wait_send()
+        for peer in range(1, halves):
             share(first, count, group, peer).wait_send()
     for distance in range(owners - 1):
         for term in range(terms):
@@ -371,7 +400,7 @@
     owners = lax.axis_size("sector")
     term_devices = lax.axis_size("term")
     capacity = max(2, 2 * blocks // owners)
-    if capacity < sectors or owners < 3:
+    if capacity < sectors or owners < 3 or term_devices % 2:
         return picked_shards(
             wavefunction,
             term_weights,
@@ -388,7 +417,8 @@
     hbm = pl.BlockSpec(memory_space=pltpu.HBM)
     smalls = (left_sector, right_sector, right_place, left_dims, right_dims, term_weights)
     bf16 = jnp.bfloat16
-    groups = (3 if early % 6 == 0 else 1) + (3 if capacity % 6 == 0 else 1)
+    counts = [n // cut for n in (early, capacity) for cut in (3 if n % 6 == 0 else 1,) for _ in range(cut)]
+    groups = len(counts)
     return pl.pallas_call(
         functools.partial(chain_kernel, owners, term_devices, early),
         out_shape=jax.ShapeDtypeStruct((blocks, rows, pad), jnp.float32),
@@ -404,13 +434,22 @@
             *[pltpu.VMEM((sectors, pad, pad), bf16) for _ in range(terms)],
             pltpu.VMEM((blocks, pad, terms * pad), bf16),
             pltpu.VMEM((capacity, pad, pad), jnp.float32),
-            pltpu.VMEM((term_devices, blocks, rows, pad), bf16),
-            pltpu.VMEM((term_devices, blocks, rows, pad), bf16),
+            pltpu.VMEM((blocks, rows, pad), jnp.float32),
+            pltpu.VMEM((term_devices // 2, blocks, rows, pad), bf16),
             pltpu.SemaphoreType.DMA((9,)),
             pltpu.SemaphoreType.DMA((2, owners - 1, terms)),
             pltpu.SemaphoreType.DMA((2, owners - 1, terms)),
-            pltpu.SemaphoreType.DMA((groups, term_devices)),
-            pltpu.SemaphoreType.DMA((groups, term_devices)),
+            pltpu.SemaphoreType.DMA((groups, term_devices // 2)),
+            pltpu.SemaphoreType.DMA((groups, term_devices // 2)),
+            *[
+                pltpu.VMEM(shape, bf16)
+                for count in counts
+                for shape in (
+                    (2, count, term_devices // 2, rows, pad),
+                    (count, term_devices // 2, rows, pad),
+                    (term_devices // 2, count, rows, pad),
+                )
+            ],
         ],
         compiler_params=pltpu.CompilerParams(
             collective_id=0, has_side_effects=True, vmem_limit_bytes=56 * 1024 * 1024

time: 50.8 us -> 50.1 us (0.986)
  Pallas kernels: 48.7 us -> 48 us
    pallas_call x1, Pallas kernels: 48.7 us -> 48 us  [shards(): pl.pallas_call(functools.partial(chain_kernel, owners, term_devices, earl...]
where the time goes in v4:
time: 50.1 us; the launch traced here: 49.9 us
  Pallas kernels  48 us (96%)
  local copies, waits for them, and re-layouts  1.92 us (4%)
    pallas_call x1, Pallas kernels, shards(): pl.pallas_call(functools.partial(chain_kernel, owners, term_devices, earl...  48 us
    unnamed x1, local copies, waits for them, and re-layouts  1.92 us

profile of v4, /device:TPU:0, one launch (start us, length us, event | category | flops | bytes accessed | tf_op | source)
XLA Modules:
  0.0 49.9 jit_solution(8339739687021674981)
XLA Ops:
  0.0 48.0 %shard_map.91 = f32[36,32,128]{2,1,0:T(8,128)} custom-call(s32[36]{0:T(128)} %left_hbm.1, s32[36]{0:T(128)} %right_hbm.1, s32[16]{0:T(128)} %place_hbm.1, s32[16]{0:T(128)} %ldim_hbm.1, s32[16]{0:T(128)} %rdim_hbm.1, f32[4,36]{1,0:T(4,128)} %weight_hbm.1, bf16[36,128,128]{2,1,0:T(8,128)(2,1)} %theta_hbm.1, bf16[4,4,128,128]{3,2,1,0:T(8,128)(2,1)} %lenv_hbm.1, ...), custom_call_target="tpu_custom_call" | custom-call | flops 1207959552 | bytes 2359296 | tf_op jit(solution)/shard_map/pallas_call | solution.py:422
  48.0 1.9 %copy.11 = f32[36,32,128]{2,1,0:T(8,128)} copy(f32[36,32,128]{2,1,0:T(8,128)} %shard_map.91) | data formatting | bytes 1179648

commit v5 on v4

--- a/solution.py
+++ b/solution.py
@@ -211,31 +211,6 @@
             return carry
         lax.fori_loop(0, count // unroll, step, 0)
 
-    each(blocks, left_product)
-
-    def is_late(block):
-        return (place_ref[right_ref[block]] // sectors == last_of(me)).astype(jnp.int32)
-
-    late_total = lax.fori_loop(0, blocks, lambda block, count: count + is_late(block), 0)
-
-    def rank(block, late_before):
-        flag = is_late(block)
-        inverse_ref[block] = jnp.where(
-            flag == 1, blocks - late_total + late_before, block - late_before
-        )
-        return late_before + flag
-
-    lax.fori_loop(0, blocks, rank, 0)
-
-    def invert(slot, carry):
-        found = 0
-        for block in range(blocks):
-            found += jnp.where(inverse_ref[block] == slot, block, 0)
-        perm_ref[slot] = found
-        return carry
-
-    lax.fori_loop(0, blocks, invert, 0)
-
     def arrive(distance, term):
         for way, step in ((0, 1), (1, -1)):
             owner = me - step * distance
@@ -254,7 +229,36 @@
                 if distance < owners - 1:
                     pass_on(far[term], owner, way, distance, term, step)
 
-    for distance in range(1, owners - 1):
+    cuts = [blocks * term // terms // unroll * unroll for term in range(terms)] + [blocks]
+    for term in range(terms):
+        each(cuts[term + 1] - cuts[term], left_product, cuts[term])
+        arrive(1, term)
+        arrive_far(1, term)
+
+    def is_late(block):
+        return (place_ref[right_ref[block]] // sectors == last_of(me)).astype(jnp.int32)
+
+    late_total = lax.fori_loop(0, blocks, lambda block, count: count + is_late(block), 0)
+
+    def rank(block, late_before):
+        flag = is_late(block)
+        inverse_ref[block] = jnp.where(
+            flag == 1, blocks - late_total + late_before, block - late_before
+        )
+        return late_before + flag
+
+    lax.fori_loop(0, blocks, rank, 0)
+
+    def invert(slot, carry):
+        found = 0
+        for block in range(blocks):
+            found += jnp.where(inverse_ref[block] == slot, block, 0)
+        perm_ref[slot] = found
+        return carry
+
+    lax.fori_loop(0, blocks, invert, 0)
+
+    for distance in range(2, owners - 1):
         for term in range(terms):
             arrive(distance, term)
             if distance < owners - 1:
@@ -452,7 +456,7 @@
             ],
         ],
         compiler_params=pltpu.CompilerParams(
-            collective_id=0, has_side_effects=True, vmem_limit_bytes=56 * 1024 * 1024
+            collective_id=0, has_side_effects=True, vmem_limit_bytes=32 * 1024 * 1024
         ),
         cost_estimate=pl.CostEstimate(
             flops=4 * blocks * terms * pad**3, bytes_accessed=4 * blocks * pad * pad, transcendentals=0

time: 50.1 us -> 55.4 us (1.11)
  local copies, waits for them, and re-layouts: 1.92 us -> 8.12 us
  Pallas kernels: 48 us -> 46.9 us
    unnamed x1 -> x19, local copies, waits for them, and re-layouts: 1.92 us -> 8.12 us
    pallas_call x1, Pallas kernels: 48 us -> 46.9 us  [shards(): pl.pallas_call(functools.partial(chain_kernel, owners, term_devices, earl...]
where the time goes in v5:
time: 55.4 us; the launch traced here: 55.1 us
  Pallas kernels  46.9 us (85%)
  local copies, waits for them, and re-layouts  8.12 us (15%)
    pallas_call x1, Pallas kernels, shards(): pl.pallas_call(functools.partial(chain_kernel, owners, term_devices, earl...  46.9 us
    unnamed x19, local copies, waits for them, and re-layouts  8.12 us

profile of v5, /device:TPU:0, one launch (start us, length us, event | category | flops | bytes accessed | tf_op | source)
XLA Modules:
  0.0 55.1 jit_solution(17468601236063561158)
XLA Ops:
  0.0 0.0 copy-start
  0.0 1.3 %copy-done = bf16[36,128,128]{2,1,0:T(8,128)(2,1)S(1)} copy-done((bf16[36,128,128]{2,1,0:T(8,128)(2,1)S(1)}, bf16[36,128,128]{2,1,0:T(8,128)(2,1)}, u32[]{:S(2)}) %copy-start) | copy-done | bytes 1179672
  1.3 0.0 copy-start.1
  1.3 1.0 %copy-done.1 = bf16[4,4,128,128]{3,2,1,0:T(8,128)(2,1)S(1)} copy-done((bf16[4,4,128,128]{3,2,1,0:T(8,128)(2,1)S(1)}, bf16[4,4,128,128]{3,2,1,0:T(8,128)(2,1)}, u32[]{:S(2)}) %copy-start.1) | copy-done | bytes 524312
  2.3 0.0 copy-start.2
  2.3 1.0 %copy-done.2 = bf16[4,4,128,128]{3,2,1,0:T(8,128)(2,1)S(1)} copy-done((bf16[4,4,128,128]{3,2,1,0:T(8,128)(2,1)S(1)}, bf16[4,4,128,128]{3,2,1,0:T(8,128)(2,1)}, u32[]{:S(2)}) %copy-start.2) | copy-done | bytes 524312
  3.4 0.0 copy-start.3
  3.4 0.7 %copy-done.3 = f32[4,36]{1,0:T(4,128)S(1)} copy-done((f32[4,36]{1,0:T(4,128)S(1)}, f32[4,36]{1,0:T(4,128)}, u32[]{:S(2)}) %copy-start.3) | copy-done | bytes 600
  4.0 0.0 copy-start.4
  4.0 0.7 %copy-done.4 = s32[36]{0:T(128)S(1)} copy-done((s32[36]{0:T(128)S(1)}, s32[36]{0:T(128)}, u32[]{:S(2)}) %copy-start.4) | copy-done | bytes 168
  4.7 0.0 copy-start.5
  4.7 0.7 %copy-done.5 = s32[36]{0:T(128)S(1)} copy-done((s32[36]{0:T(128)S(1)}, s32[36]{0:T(128)}, u32[]{:S(2)}) %copy-start.5) | copy-done | bytes 168
  5.3 0.0 copy-start.6
  5.4 0.7 %copy-done.6 = s32[16]{0:T(128)S(1)} copy-done((s32[16]{0:T(128)S(1)}, s32[16]{0:T(128)}, u32[]{:S(2)}) %copy-start.6) | copy-done | bytes 88
  6.0 0.0 copy-start.7
  6.0 0.7 %copy-done.7 = s32[16]{0:T(128)S(1)} copy-done((s32[16]{0:T(128)S(1)}, s32[16]{0:T(128)}, u32[]{:S(2)}) %copy-start.7) | copy-done | bytes 88
  6.7 0.0 copy-start.8
  6.7 0.7 %copy-done.8 = s32[16]{0:T(128)S(1)} copy-done((s32[16]{0:T(128)S(1)}, s32[16]{0:T(128)}, u32[]{:S(2)}) %copy-start.8) | copy-done | bytes 88
  7.3 46.9 %shard_map.91 = f32[36,32,128]{2,1,0:T(8,128)S(1)} custom-call(s32[36]{0:T(128)S(1)} %copy-done.4, s32[36]{0:T(128)S(1)} %copy-done.5, s32[16]{0:T(128)S(1)} %copy-done.6, s32[16]{0:T(128)S(1)} %copy-done.7, s32[16]{0:T(128)S(1)} %copy-done.8, f32[4,36]{1,0:T(4,128)S(1)} %copy-done.3, bf16[36,128,128]{2,1,0:T(8,128)(2,1)S(1)} %copy-done, ...), custom_call_target="tpu_custom_call" | custom-call | flops 1207959552 | bytes 2359296 | tf_op jit(solution)/shard_map/pallas_call | solution.py:426
  54.3 0.8 %copy.11 = f32[36,32,128]{2,1,0:T(8,128)} copy(f32[36,32,128]{2,1,0:T(8,128)S(1)} %shard_map.91) | data formatting | bytes 1179648
Async XLA Ops:
  0.0 1.3 %copy-start = (bf16[36,128,128]{2,1,0:T(8,128)(2,1)S(1)}, bf16[36,128,128]{2,1,0:T(8,128)(2,1)}, u32[]{:S(2)}) copy-start(bf16[36,128,128]{2,1,0:T(8,128)(2,1)} %theta_hbm.1) | copy-start | bytes 3538948
  1.3 1.0 %copy-start.1 = (bf16[4,4,128,128]{3,2,1,0:T(8,128)(2,1)S(1)}, bf16[4,4,128,128]{3,2,1,0:T(8,128)(2,1)}, u32[]{:S(2)}) copy-start(bf16[4,4,128,128]{3,2,1,0:T(8,128)(2,1)} %lenv_hbm.1) | copy-start | bytes 1572868
  2.3 1.0 %copy-start.2 = (bf16[4,4,128,128]{3,2,1,0:T(8,128)(2,1)S(1)}, bf16[4,4,128,128]{3,2,1,0:T(8,128)(2,1)}, u32[]{:S(2)}) copy-start(bf16[4,4,128,128]{3,2,1,0:T(8,128)(2,1)} %renv_hbm.1) | copy-start | bytes 1572868
  3.4 0.7 %copy-start.3 = (f32[4,36]{1,0:T(4,128)S(1)}, f32[4,36]{1,0:T(4,128)}, u32[]{:S(2)}) copy-start(f32[4,36]{1,0:T(4,128)} %weight_hbm.1) | copy-start | bytes 1732
  4.0 0.7 %copy-start.4 = (s32[36]{0:T(128)S(1)}, s32[36]{0:T(128)}, u32[]{:S(2)}) copy-start(s32[36]{0:T(128)} %left_hbm.1) | copy-start | bytes 436
  4.7 0.7 %copy-start.5 = (s32[36]{0:T(128)S(1)}, s32[36]{0:T(128)}, u32[]{:S(2)}) copy-start(s32[36]{0:T(128)} %right_hbm.1) | copy-start | bytes 436
  5.3 0.7 %copy-start.6 = (s32[16]{0:T(128)S(1)}, s32[16]{0:T(128)}, u32[]{:S(2)}) copy-start(s32[16]{0:T(128)} %place_hbm.1) | copy-start | bytes 196
  6.0 0.7 %copy-start.7 = (s32[16]{0:T(128)S(1)}, s32[16]{0:T(128)}, u32[]{:S(2)}) copy-start(s32[16]{0:T(128)} %ldim_hbm.1) | copy-start | bytes 196
  6.7 0.7 %copy-start.8 = (s32[16]{0:T(128)S(1)}, s32[16]{0:T(128)}, u32[]{:S(2)}) copy-start(s32[16]{0:T(128)} %rdim_hbm.1) | copy-start | bytes 196

commit v6 on v5

--- a/solution.py
+++ b/solution.py
@@ -456,7 +456,7 @@
             ],
         ],
         compiler_params=pltpu.CompilerParams(
-            collective_id=0, has_side_effects=True, vmem_limit_bytes=32 * 1024 * 1024
+            collective_id=0, has_side_effects=True, vmem_limit_bytes=56 * 1024 * 1024
         ),
         cost_estimate=pl.CostEstimate(
             flops=4 * blocks * terms * pad**3, bytes_accessed=4 * blocks * pad * pad, transcendentals=0

time: 55.4 us -> 50.1 us (0.904)
  local copies, waits for them, and re-layouts: 8.12 us -> 1.92 us
  Pallas kernels: 46.9 us -> 48 us
    unnamed x19 -> x1, local copies, waits for them, and re-layouts: 8.12 us -> 1.92 us
    pallas_call x1, Pallas kernels: 46.9 us -> 48 us  [shards(): pl.pallas_call(functools.partial(chain_kernel, owners, term_devices, earl...]
where the time goes in v6:
time: 50.1 us; the launch traced here: 49.9 us
  Pallas kernels  48 us (96%)
  local copies, waits for them, and re-layouts  1.92 us (4%)
    pallas_call x1, Pallas kernels, shards(): pl.pallas_call(functools.partial(chain_kernel, owners, term_devices, earl...  48 us
    unnamed x1, local copies, waits for them, and re-layouts  1.92 us

profile of v6, /device:TPU:0, one launch (start us, length us, event | category | flops | bytes accessed | tf_op | source)
XLA Modules:
  0.0 49.9 jit_solution(2971761915045097539)
XLA Ops:
  0.0 48.0 %shard_map.91 = f32[36,32,128]{2,1,0:T(8,128)} custom-call(s32[36]{0:T(128)} %left_hbm.1, s32[36]{0:T(128)} %right_hbm.1, s32[16]{0:T(128)} %place_hbm.1, s32[16]{0:T(128)} %ldim_hbm.1, s32[16]{0:T(128)} %rdim_hbm.1, f32[4,36]{1,0:T(4,128)} %weight_hbm.1, bf16[36,128,128]{2,1,0:T(8,128)(2,1)} %theta_hbm.1, bf16[4,4,128,128]{3,2,1,0:T(8,128)(2,1)} %lenv_hbm.1, ...), custom_call_target="tpu_custom_call" | custom-call | flops 1207959552 | bytes 2359296 | tf_op jit(solution)/shard_map/pallas_call | solution.py:426
  48.0 1.9 %copy.11 = f32[36,32,128]{2,1,0:T(8,128)} copy(f32[36,32,128]{2,1,0:T(8,128)} %shard_map.91) | data formatting | bytes 1179648
